TPU v7x, 32 devices: a whole 2x2x4 slice. The times are simulated.
32 devices in a mesh: dp: 4 (over z), expert: 4 (over y, x), tensor: 2 (over core).
Axes of the slice: x: 2, y: 2, z: 4, core: 2. Of those that a mesh axis runs over, the one named last changes fastest.
Arguments:
- hidden_in: bfloat16 [4096, 2048], P(('dp', 'expert')), may hold values from -6 to 6
- query: bfloat16 [4096, 2048], P(('dp', 'expert'), 'tensor'), may hold values from -26 to 26
- keys: bfloat16 [4096, 2048], P(('dp', 'expert'), 'tensor'), may hold values from -26 to 26
- values: bfloat16 [4096, 2048], P(('dp', 'expert'), 'tensor'), may hold values from -6 to 6
- out_proj: bfloat16 [2048, 2048], P('tensor'), may hold values from -0.125 to 0.125
- norm_gain: bfloat16 [2048], replicated, may hold values from 0.25 to 1.75
- routes: int32 [4096, 2], P(('dp', 'expert')), may hold values from 0 to 3, all different within a row; in each aligned block of 256 rows (0 to 255, 256 to 511, ...) at most 144 rows name the same one
- gates: float32 [4096, 2], P(('dp', 'expert')), may hold values from 0.2 to 1
- w_gate: bfloat16 [4, 2048, 5504], P('expert', 'dp', 'tensor'), may hold values from -0.125 to 0.125
- w_up: bfloat16 [4, 2048, 5504], P('expert', 'dp', 'tensor'), may hold values from -0.125 to 0.125
- w_down_t: bfloat16 [4, 2048, 5504], P('expert', 'dp', 'tensor'), may hold values from -0.078125 to 0.078125
Outputs:
- layer_out: bfloat16 [4096, 2048], P(('dp', 'expert'), 'tensor')
Inputs may be any that keep to these rules, and one draw needn't show every extreme that they name: `routes`: each row names 2 different experts; in the 256 rows of one block of consecutive tokens no expert is named more than 144 times, a bound that some block reaches.
All inputs are finite; a program needn't handle non-finite values.
Results may differ from a plain program's by a relative error of at most 0.0095.
Values may be sent and summed in bfloat16 or wider, within the bound.
A program may use at most 128 MiB of HBM per device.

v0:
```python
import jax
import jax.numpy as jnp
from jax import lax
from jax.sharding import PartitionSpec as P

HDIM = 128
EPSILON = 1e-05
NEGATIVE = -1e30


def slot_table(block_routes, experts, capacity):
    flat_routes = block_routes.reshape(-1)
    pairs = flat_routes.shape[0]
    onehot = flat_routes[:, None] == jnp.arange(experts, dtype=jnp.int32)[None, :]
    order = jnp.arange(pairs, dtype=jnp.int32)
    earlier = (order[:, None] > order[None, :]).astype(jnp.bfloat16)
    rank_table = jnp.dot(earlier, onehot.astype(jnp.bfloat16), preferred_element_type=jnp.float32)
    slot_index = jnp.sum(jnp.where(onehot, rank_table, 0.0), axis=1).astype(jnp.int32)
    return flat_routes * capacity + slot_index


def attention(query, both, score_scale):
    tok_rows, head_cols = query.shape
    head_count = head_cols // HDIM
    query_pos = lax.axis_index("expert") * tok_rows + jnp.arange(tok_rows, dtype=jnp.int32)
    key_rows, value_rows = (both[:, :head_cols], both[:, head_cols:])
    count_rows = key_rows.shape[0]
    key_pos = jnp.arange(count_rows, dtype=jnp.int32)
    queries = query.reshape(tok_rows, head_count, HDIM)
    key_part = key_rows.reshape(count_rows, head_count, HDIM)
    value_part = value_rows.reshape(count_rows, head_count, HDIM)
    scores = (
        jnp.einsum("qhd,khd->hqk", queries, key_part, preferred_element_type=jnp.float32)
        * score_scale
    )
    causal = (query_pos[:, None] >= key_pos[None, :])[None]
    scores = jnp.where(causal, scores, NEGATIVE)
    new_max = jnp.max(scores, axis=-1)
    weights_now = jnp.where(causal, jnp.exp(scores - new_max[..., None]), 0.0)
    totals = jnp.sum(weights_now, axis=-1)
    weighted = jnp.einsum("hqk,khd->hqd", weights_now, value_part.astype(jnp.float32))
    context = weighted / totals[..., None]
    return jnp.transpose(context, (1, 0, 2)).reshape(tok_rows, head_cols).astype(jnp.bfloat16)


def local(
    hidden_in, query, keys, values, out_proj, norm_gain, routes, gates, w_gate, w_up, w_down_t
):
    tok_rows, feature_width = hidden_in.shape
    top = routes.shape[1]
    experts = lax.axis_size("expert")
    copies = lax.axis_size("dp")
    capacity = 9 * tok_rows // (4 * experts)
    slots = experts * capacity
    tensor_count = lax.axis_size("tensor")
    slice_width = feature_width // tensor_count
    tensor_index = lax.axis_index("tensor")
    shard_rows, hidden_width = w_gate.shape[1:]
    exchange = 2 * tok_rows * feature_width < 3 * shard_rows * hidden_width and copies <= 4
    if hidden_width % copies:
        exchange = False

    def spread(w):
        if not exchange:
            return lax.all_gather(w[0], "dp", axis=0, tiled=True)
        share = hidden_width // copies
        me = lax.axis_index("dp")
        turned = jnp.transpose(w[0]).reshape(copies, share, shard_rows)
        blocks = []
        for step in range(copies):
            block = lax.dynamic_index_in_dim(turned, (me + step) % copies, 0, keepdims=False)
            if step:
                block = lax.ppermute(block, "dp", [(i, (i + step) % copies) for i in range(copies)])
            blocks.append(block)
        stacked = jnp.stack(blocks)
        ordered = [
            lax.dynamic_index_in_dim(stacked, (me - i + copies) % copies, 0, keepdims=False)
            for i in range(copies)
        ]
        return jnp.transpose(jnp.concatenate(ordered, axis=1))

    choice = jnp.concatenate([routes.astype(jnp.float32), gates], axis=1)
    both = lax.all_gather(jnp.concatenate([keys, values], axis=1), "expert", axis=0, tiled=True)
    if exchange:
        choice = lax.all_gather(choice, "dp", axis=0)
        choice, w_gate, w_up, w_down_t = lax.optimization_barrier((choice, w_gate, w_up, w_down_t))
    else:
        choice = choice[None]
    gate_full, up_full, down_full = (spread(w_gate), spread(w_up), spread(w_down_t))
    if exchange:
        both, gate_full = lax.optimization_barrier((both, gate_full))
    context = attention(query, both, 1.0 / HDIM**0.5)
    attended = lax.psum(
        jnp.dot(context, out_proj, preferred_element_type=jnp.float32).astype(jnp.bfloat16),
        "tensor",
    )
    if exchange:
        attended, up_full = lax.optimization_barrier((attended, up_full))
    attended = attended.astype(jnp.float32)
    residual = hidden_in.astype(jnp.float32) + attended
    mean_square = jnp.mean(residual * residual, axis=-1, keepdims=True)
    normed = (residual * lax.rsqrt(mean_square + EPSILON) * norm_gain.astype(jnp.float32)).astype(
        jnp.bfloat16
    )
    own_cols = lax.dynamic_slice_in_dim(normed, tensor_index * slice_width, slice_width, 1)
    own_slice = lax.dynamic_slice_in_dim(residual, tensor_index * slice_width, slice_width, 1)
    blocks = lax.all_gather(own_cols, "dp", axis=0) if exchange else own_cols[None]
    count = blocks.shape[0]
    sends, mixers = ([], [])
    slot_numbers = jnp.arange(slots, dtype=jnp.int32)[:, None]
    for i in range(count):
        picked = choice[i, :, :top].astype(jnp.int32)
        targets = slot_table(picked, experts, capacity).reshape(tok_rows, top)
        place = jnp.zeros((slots, tok_rows), jnp.float32)
        mixing = jnp.zeros((slots, tok_rows), jnp.float32)
        for k in range(top):
            chosen = slot_numbers == targets[:, k][None, :]
            place = jnp.where(chosen, 1.0, place)
            mixing = jnp.where(chosen, choice[i, :, top + k][None, :], mixing)
        sent = jnp.dot(
            place.astype(jnp.bfloat16), blocks[i], preferred_element_type=jnp.float32
        ).astype(jnp.bfloat16)
        sends.append(sent.reshape(experts, capacity, slice_width))
        mixers.append(mixing)
    arrived = lax.all_to_all(
        jnp.concatenate(sends, axis=1), "expert", split_axis=0, concat_axis=0, tiled=True
    ).reshape(count * slots, slice_width)
    if exchange:
        arrived, down_full = lax.optimization_barrier((arrived, down_full))
    halves = lax.all_gather(arrived, "tensor", axis=0)
    slot_rows = jnp.concatenate([halves[i] for i in range(tensor_count)], axis=1)
    gate_out = jnp.dot(slot_rows, gate_full, preferred_element_type=jnp.float32)
    up_out = jnp.dot(slot_rows, up_full, preferred_element_type=jnp.float32)
    hidden = (jax.nn.silu(gate_out) * up_out).astype(jnp.bfloat16)
    hidden = lax.optimization_barrier(hidden)
    parts = 2 if slice_width % 256 == 0 else 1
    width = slice_width // parts
    down_parts = down_full.reshape(tensor_count, parts, width, down_full.shape[1])
    splits = [(mixing, lax.reduce_precision(mixing, 8, 7)) for mixing in mixers]
    pieces = []
    for part in range(parts):
        rounded = lax.dot_general(
            hidden,
            down_parts[:, part].reshape(tensor_count * width, down_full.shape[1]),
            (((1,), (1,)), ((), ())),
            preferred_element_type=jnp.float32,
        ).astype(jnp.bfloat16)
        summed = lax.psum_scatter(rounded, "tensor", scatter_dimension=1, tiled=True)
        returned = lax.all_to_all(
            summed.reshape(experts, count * capacity, width),
            "expert",
            split_axis=0,
            concat_axis=0,
            tiled=True,
        )
        mixtures = []
        for i, (mixing, high) in enumerate(splits):
            rows = returned[:, i * capacity : (i + 1) * capacity].reshape(slots, width)
            mixtures.append(
                sum(
                    (
                        lax.dot_general(
                            term.astype(jnp.bfloat16),
                            rows,
                            (((0,), (0,)), ((), ())),
                            preferred_element_type=jnp.float32,
                        )
                        for term in (high, mixing - high)
                    )
                )
            )
        if exchange:
            piece = lax.psum_scatter(
                jnp.concatenate(mixtures, axis=0).astype(jnp.bfloat16),
                "dp",
                scatter_dimension=0,
                tiled=True,
            ).astype(jnp.float32)
        else:
            piece = mixtures[0]
        pieces.append(piece)
    mixture = jnp.concatenate(pieces, axis=1)
    return (own_slice + mixture).astype(jnp.bfloat16)


def solution(mesh):
    in_specs = (
        P(("dp", "expert"), None),
        P(("dp", "expert"), "tensor"),
        P(("dp", "expert"), "tensor"),
        P(("dp", "expert"), "tensor"),
        P("tensor", None),
        P(),
        P(("dp", "expert"), None),
        P(("dp", "expert"), None),
        P("expert", "dp", "tensor"),
        P("expert", "dp", "tensor"),
        P("expert", "dp", "tensor"),
    )
    out_specs = P(("dp", "expert"), "tensor")
    return jax.shard_map(local, mesh=mesh, in_specs=in_specs, out_specs=out_specs, check_vma=False)
```

profile of v0, /device:TPU:0, one launch (start us, length us, event | category | flops | bytes accessed | tf_op | source)
XLA Modules:
  0.0 471.7 jit_solution(1408861958945248297)
XLA Ops:
  6.5 1.3 copy.21
  7.9 1.2 copy.22
  9.1 1.0 pad_maximum_fusion.9
  10.3 14.8 %all-gather = f32[1024,4]{0,1:T(4,128)S(1)} all-gather(f32[256,4]{0,1:T(4,128)S(1)} %pad_maximum_fusion.12), channel_id=2, replica_groups=mesh['dp'=4,'expert'=4,'tensor'=2] {'dp'}, dimensions={0}, use_global_device_ids=true | all-gather | bytes 20480 | tf_op jit(solution)/shard_map/all_gather | solution.py:85
  25.4 3.4 constant_dynamic-slice_fusion.2
  28.8 3.4 collective-permute-start.2
  32.2 0.6 collective-permute-start
  32.7 1.4 constant_dynamic-slice_fusion.1
  34.1 3.3 collective-permute-start.5
  37.4 1.1 collective-permute-start.4
  38.7 11.5 %collective-permute-done.2 = bf16[688,512]{1,0:T(8,128)(2,1)} collective-permute-done((bf16[688,512]{1,0:T(8,128)(2,1)}, bf16[688,512]{1,0:T(8,128)(2,1)}, u32[]{:S(2)}, u32[]{:S(2)}) %collective-permute-start.2) | collective-permute-done | bytes 704544 | tf_op jit(solution)/shard_map/ppermute | solution.py:73
  50.2 29.1 %collective-permute-start.3 = (bf16[688,512]{1,0:T(8,128)(2,1)S(1)}, bf16[688,512]{1,0:T(8,128)(2,1)}, u32[]{:S(2)}, u32[]{:S(2)}) collective-permute-start(bf16[688,512]{1,0:T(8,128)(2,1)S(1)} %get-tuple-element.62), channel_id=1, source_target_pairs={{0,8},{8,16},{16,24},{24,0},{1,9},{9,17},{17,25},{25,1},{2,10},{10... | collective-permute-start | bytes 2113544 | tf_op jit(solution)/shard_map/ppermute | solution.py:73
  79.2 45.1 %collective-permute-done.1 = bf16[688,512]{1,0:T(8,128)(2,1)} collective-permute-done((bf16[688,512]{1,0:T(8,128)(2,1)}, bf16[688,512]{1,0:T(8,128)(2,1)}, u32[]{:S(2)}, u32[]{:S(2)}) %collective-permute-start.1) | collective-permute-done | bytes 704544 | tf_op jit(solution)/shard_map/ppermute | solution.py:73
  124.4 1.7 pad_maximum_fusion.4
  126.3 1.7 maximum_bitcast_fusion
  128.0 2.7 fusion.100
  130.7 1.7 fusion
  132.5 2.0 fusion.3
  134.5 2.3 divide_convert_fusion
  136.8 2.3 convolution_convert_fusion.2
  139.5 11.1 %collective-permute-done.4 = bf16[688,512]{1,0:T(8,128)(2,1)} collective-permute-done((bf16[688,512]{1,0:T(8,128)(2,1)}, bf16[688,512]{1,0:T(8,128)(2,1)}, u32[]{:S(2)}, u32[]{:S(2)}) %collective-permute-start.4) | collective-permute-done | bytes 704544 | tf_op jit(solution)/shard_map/ppermute | solution.py:73
  150.6 1.7 pad_maximum_fusion.5
  152.5 1.8 maximum_bitcast_fusion.1
  154.3 2.8 all-reduce.2.cloned.1.call-done
  157.1 1.6 multiply_reduce_fusion
  158.8 1.3 copy-done.5
  160.1 0.9 multiply_convert_fusion.1
  164.1 44.2 %all-gather.9.cloned.1.call-done = bf16[1024,1024]{1,0:T(8,128)(2,1)} async-done(((bf16[256,1024]{1,0:T(8,128)(2,1)}), bf16[1024,1024]{1,0:T(8,128)(2,1)}) %all-gather.9.cloned.1.call-update) | async-done | bytes 2097168 | tf_op jit(solution)/shard_map/all_gather | solution.py:107
  208.3 1.7 convolution_convert_fusion.4
  210.0 1.5 convolution_convert_fusion.5
  211.5 0.5 convolution_convert_fusion.6
  212.0 0.5 convolution_convert_fusion.3
  212.5 2.4 pad_maximum_fusion.3
  214.8 5.2 %all-to-all-start = ((bf16[4,576,1024]{2,1,0:T(8,128)(2,1)}), bf16[4,576,1024]{2,1,0:T(8,128)(2,1)}, u32[]{:S(2)}, u32[]{:S(2)}) async-start(bf16[4,576,1024]{2,1,0:T(8,128)(2,1)} %pad_maximum_fusion.3), calls=%async_computation | async-start | bytes 9437184 | tf_op jit(solution)/shard_map/all_to_all | solution.py:125
  220.3 1.2 collective-permute-start.8
  221.7 1.7 collective-permute-start.6
  223.5 15.5 %collective-permute-done.8 = bf16[688,512]{1,0:T(8,128)(2,1)S(1)} collective-permute-done((bf16[688,512]{1,0:T(8,128)(2,1)S(1)}, bf16[688,512]{1,0:T(8,128)(2,1)S(1)}, u32[]{:S(2)}, u32[]{:S(2)}) %collective-permute-start.8) | collective-permute-done | bytes 704544 | tf_op jit(solution)/shard_map/ppermute | solution.py:73
  238.9 43.6 %collective-permute-done.7 = bf16[688,512]{1,0:T(8,128)(2,1)S(1)} collective-permute-done((bf16[688,512]{1,0:T(8,128)(2,1)S(1)}, bf16[688,512]{1,0:T(8,128)(2,1)S(1)}, u32[]{:S(2)}, u32[]{:S(2)}) %collective-permute-start.7) | collective-permute-done | bytes 704544 | tf_op jit(solution)/shard_map/ppermute | solution.py:73
  283.1 1.8 maximum_bitcast_fusion.2
  285.0 0.6 reduce-scatter.5.cloned.1.call-start
  285.5 6.5 %reshape.189 = bf16[2,2,512,688]{2,1,0,3:T(2,128)(2,1)S(1)} reshape(bf16[2048,688]{0,1:T(8,128)(2,1)} %maximum_bitcast_fusion.2) | data formatting | bytes 5636096 | tf_op jit(solution)/shard_map/reshape | solution.py:138
  292.1 19.3 %slice_reduce_fusion.1 = (bf16[2,512,688]{1,0,2:T(2,128)(2,1)S(1)}, bf16[2,512,688]{1,0,2:T(2,128)(2,1)}) fusion(bf16[2,2,512,688]{2,1,0,3:T(2,128)(2,1)S(1)} %reshape.189), kind=kLoop, calls=%fused_computation.18 | loop fusion | bytes 5636096 | tf_op jit(solution)/shard_map/slice | solution.py:144
  311.4 1.5 copy.30
  312.9 7.3 %fusion.99 = (bf16[2304,1024]{1,0:T(8,128)(2,1)S(1)}, bf16[2304,1024]{1,0:T(8,128)(2,1)}) fusion(bf16[4608,1024]{1,0:T(8,128)(2,1)} %all-gather.11.cloned.1.call-done), kind=kLoop, calls=%fused_computation.212 | loop fusion | bytes 18874368 | tf_op jit(solution)/shard_map/slice | solution.py:131
  320.2 11.6 %fusion.1 = f32[2304,688]{0,1:T(8,128)} fusion(bf16[2048,688]{0,1:T(8,128)(2,1)S(1)} %copy-done.12, bf16[2304,1024]{1,0:T(8,128)(2,1)} %get-tuple-element.44, bf16[2304,1024]{1,0:T(8,128)(2,1)S(1)} %get-tuple-element.43), kind=kOutput, calls=%fused_computation.5 | convolution fusion | flops 6511656960 | bytes 18595840 | tf_op jit(solution)/shard_map/dot_general | solution.py:133
  331.7 9.6 %multiply_convert_fusion = bf16[2304,688]{0,1:T(8,128)(2,1)S(1)} fusion(f32[2304,688]{0,1:T(8,128)} %fusion.1, bf16[2048,688]{0,1:T(8,128)(2,1)S(1)} %copy-done.11, bf16[2304,1024]{1,0:T(8,128)(2,1)S(1)} %copy-done.8, bf16[2304,1024]{1,0:T(8,128)(2,1)S(1)} %get-tuple-element.43), kind=kOutput, calls=%fused_computation.4 | convolution fusion | flops 6521167872 | bytes 21766144 | tf_op jit(solution)/shard_map/dot_general | solution.py:132
  341.4 1.6 copy-done.20
  343.0 5.5 %convolution_convert_fusion.1 = bf16[2304,1024]{1,0:T(8,128)(2,1)} fusion(bf16[2304,688]{0,1:T(8,128)(2,1)S(1)} %multiply_convert_fusion, bf16[1024,688]{0,1:T(8,128)(2,1)S(1)} %bitcast.174), kind=kOutput, calls=%fused_computation.10 | convolution fusion | flops 3248750592 | bytes 9297920 | tf_op jit(solution)/shard_map/dot_general | solution.py:142
  348.6 1.3 copy-done.7
  350.2 7.6 %convolution_convert_fusion = bf16[2304,1024]{1,0:T(8,128)(2,1)} fusion(bf16[2304,688]{0,1:T(8,128)(2,1)} %copy-done.20, bf16[1024,688]{0,1:T(8,128)(2,1)S(1)} %bitcast.175), kind=kOutput, calls=%fused_computation.9 | convolution fusion | flops 3248750592 | bytes 9297920 | tf_op jit(solution)/shard_map/dot_general | solution.py:142
  357.8 4.2 reduce-scatter.5.cloned.1.call-done
  362.0 3.9 all-to-all-start.1
  365.9 0.7 slice_reduce_fusion.17
  366.6 11.4 %reduce-scatter.9.cloned.1.call-done = bf16[2304,512]{1,0:T(8,128)(2,1)} async-done(((bf16[2304,1024]{1,0:T(8,128)(2,1)}), bf16[2304,512]{1,0:T(8,128)(2,1)}) %reduce-scatter.9.cloned.1.call-update) | async-done | bytes 2359312 | tf_op jit(solution)/shard_map/reduce_scatter | solution.py:148
  378.0 16.1 %all-to-all-done.1 = bf16[4,576,512]{2,1,0:T(8,128)(2,1)S(1)} async-done(((bf16[4,576,512]{2,1,0:T(8,128)(2,1)}), bf16[4,576,512]{2,1,0:T(8,128)(2,1)S(1)}, u32[]{:S(2)}, u32[]{:S(2)}) %all-to-all-start.1) | async-done | bytes 2359328 | tf_op jit(solution)/shard_map/all_to_all | solution.py:149
  394.1 1.4 copy-done.4
  395.5 3.6 all-to-all-start.2
  399.4 1.8 fusion.101
  404.6 1.1 pad_maximum_fusion.10
  405.7 20.7 %all-to-all-done.2 = bf16[4,576,512]{2,1,0:T(8,128)(2,1)S(1)} async-done(((bf16[4,576,512]{2,1,0:T(8,128)(2,1)}), bf16[4,576,512]{2,1,0:T(8,128)(2,1)S(1)}, u32[]{:S(2)}, u32[]{:S(2)}) %all-to-all-start.2) | async-done | bytes 2359328 | tf_op jit(solution)/shard_map/all_to_all | solution.py:149
  430.0 1.1 pad_maximum_fusion.11
  431.1 3.4 reduce-scatter.7.cloned.1.call-done
  434.5 28.1 %reduce-scatter.11.cloned.1.call-done = bf16[256,512]{1,0:T(8,128)(2,1)} async-done(((bf16[1024,512]{1,0:T(8,128)(2,1)}), bf16[256,512]{1,0:T(8,128)(2,1)}) %reduce-scatter.11.cloned.1.call-update) | async-done | bytes 262160 | tf_op jit(solution)/shard_map/reduce_scatter | solution.py:173
  462.7 2.0 add_convert_fusion
  (112 shorter events, 12.8 us)
Async XLA Ops:
  6.5 124.2 %copy-start = (bf16[256,1024]{1,0:T(8,128)(2,1)S(1)}, bf16[256,1024]{1,0:T(8,128)(2,1)}, u32[]{:S(2)}) copy-start(bf16[256,1024]{1,0:T(8,128)(2,1)} %param.12) | copy-start | bytes 1572868
  6.5 3.7 copy-start.16
  6.5 3.8 copy-start.17
  6.5 121.5 %all-gather.7.cloned.1.call-start = ((), (), s32[]{:S(2)}) async-start(), calls=%async_computation.7 | async-start | bytes 5242880 | tf_op jit(solution)/shard_map/all_gather | solution.py:83
  10.2 146.9 %all-reduce.2.cloned.1.call-start = ((), (), s32[]{:S(2)}) async-start(), calls=%async_computation.8 | async-start | bytes 2097152 | tf_op jit(solution)/shard_map/psum | solution.py:93
  25.4 138.0 %copy-start.2 = (f32[1024,4]{1,0:T(8,128)}, f32[1024,4]{1,0:T(8,128)S(1)}, u32[]{:S(2)}) copy-start(f32[1024,4]{1,0:T(8,128)S(1)} %copy.23) | copy-start | bytes 49156
  25.4 7.3 %copy-start.9 = (bf16[1,512,2752]{1,2,0:T(8,128)(2,1)S(1)}, bf16[1,512,2752]{1,2,0:T(8,128)(2,1)}, u32[]{:S(2)}) copy-start(bf16[1,512,2752]{1,2,0:T(8,128)(2,1)} %param.20) | copy-start | bytes 8454148
  28.8 21.4 %collective-permute-start.2 = (bf16[688,512]{1,0:T(8,128)(2,1)}, bf16[688,512]{1,0:T(8,128)(2,1)}, u32[]{:S(2)}, u32[]{:S(2)}) collective-permute-start(bf16[688,512]{1,0:T(8,128)(2,1)} %get-tuple-element.68), channel_id=1, source_target_pairs={{0,24},{8,0},{16,8},{24,16},{1,25},{9,1},{17,9},{25,17},{2,26},{10... | collective-permute-start | bytes 2113544 | tf_op jit(solution)/shard_map/ppermute | solution.py:73
  32.2 92.2 %collective-permute-start.1 = (bf16[688,512]{1,0:T(8,128)(2,1)}, bf16[688,512]{1,0:T(8,128)(2,1)}, u32[]{:S(2)}, u32[]{:S(2)}) collective-permute-start(bf16[688,512]{1,0:T(8,128)(2,1)} %get-tuple-element.69), channel_id=1, source_target_pairs={{0,16},{8,24},{16,0},{24,8},{1,17},{9,25},{17,1},{25,9},{2,18},{10... | collective-permute-start | bytes 2113544 | tf_op jit(solution)/shard_map/ppermute | solution.py:73
  32.2 92.2 %collective-permute-start = (bf16[688,512]{1,0:T(8,128)(2,1)}, bf16[688,512]{1,0:T(8,128)(2,1)}, u32[]{:S(2)}, u32[]{:S(2)}) collective-permute-start(bf16[688,512]{1,0:T(8,128)(2,1)} %get-tuple-element.70), channel_id=1, source_target_pairs={{0,8},{8,16},{16,24},{24,0},{1,9},{9,17},{17,25},{25,1},{2,10},{10... | collective-permute-start | bytes 2113544 | tf_op jit(solution)/shard_map/ppermute | solution.py:73
  34.1 105.4 %collective-permute-start.5 = (bf16[688,512]{1,0:T(8,128)(2,1)}, bf16[688,512]{1,0:T(8,128)(2,1)}, u32[]{:S(2)}, u32[]{:S(2)}) collective-permute-start(bf16[688,512]{1,0:T(8,128)(2,1)} %get-tuple-element.60), channel_id=1, source_target_pairs={{0,24},{8,0},{16,8},{24,16},{1,25},{9,1},{17,9},{25,17},{2,26},{10... | collective-permute-start | bytes 2113544 | tf_op jit(solution)/shard_map/ppermute | solution.py:73
  37.4 113.2 %collective-permute-start.4 = (bf16[688,512]{1,0:T(8,128)(2,1)}, bf16[688,512]{1,0:T(8,128)(2,1)}, u32[]{:S(2)}, u32[]{:S(2)}) collective-permute-start(bf16[688,512]{1,0:T(8,128)(2,1)} %get-tuple-element.61), channel_id=1, source_target_pairs={{0,16},{8,24},{16,0},{24,8},{1,17},{9,25},{17,1},{25,9},{2,18},{10... | collective-permute-start | bytes 2113544 | tf_op jit(solution)/shard_map/ppermute | solution.py:73
  50.2 100.4 %collective-permute-start.3 = (bf16[688,512]{1,0:T(8,128)(2,1)S(1)}, bf16[688,512]{1,0:T(8,128)(2,1)}, u32[]{:S(2)}, u32[]{:S(2)}) collective-permute-start(bf16[688,512]{1,0:T(8,128)(2,1)S(1)} %get-tuple-element.62), channel_id=1, source_target_pairs={{0,8},{8,16},{16,24},{24,0},{1,9},{9,17},{17,25},{25,1},{2,10},{10... | collective-permute-start | bytes 2113544 | tf_op jit(solution)/shard_map/ppermute | solution.py:73
  134.5 2.3 copy-start.18
  136.8 2.7 copy-start.15
  139.1 69.2 %all-gather.9.cloned.1.call-start = ((), (), s32[]{:S(2)}) async-start(), calls=%async_computation.13 | async-start | bytes 2621440 | tf_op jit(solution)/shard_map/all_gather | solution.py:107
  152.5 4.6 copy-start.14
  158.7 1.3 copy-start.5
  208.3 3.2 copy-start.19
  214.8 5.2 %copy-start.10 = (bf16[1,512,2752]{1,2,0:T(8,128)(2,1)S(1)}, bf16[1,512,2752]{1,2,0:T(8,128)(2,1)}, u32[]{:S(2)}) copy-start(bf16[1,512,2752]{1,2,0:T(8,128)(2,1)} %param.21) | copy-start | bytes 8454148
  214.8 70.1 %all-to-all-start = ((bf16[4,576,1024]{2,1,0:T(8,128)(2,1)}), bf16[4,576,1024]{2,1,0:T(8,128)(2,1)}, u32[]{:S(2)}, u32[]{:S(2)}) async-start(bf16[4,576,1024]{2,1,0:T(8,128)(2,1)} %pad_maximum_fusion.3), calls=%async_computation | async-start | bytes 9437184 | tf_op jit(solution)/shard_map/all_to_all | solution.py:125
  220.0 92.9 %all-gather.11.cloned.1.call-start = ((), (), s32[]{:S(2)}) async-start(), calls=%async_computation.14 | async-start | bytes 14155776 | tf_op jit(solution)/shard_map/all_gather | solution.py:130
  220.3 18.6 %collective-permute-start.8 = (bf16[688,512]{1,0:T(8,128)(2,1)S(1)}, bf16[688,512]{1,0:T(8,128)(2,1)S(1)}, u32[]{:S(2)}, u32[]{:S(2)}) collective-permute-start(bf16[688,512]{1,0:T(8,128)(2,1)S(1)} %get-tuple-element.52), channel_id=1, source_target_pairs={{0,24},{8,0},{16,8},{24,16},{1,25},{9,1},{17,9},{25,17},{2,26},{10... | collective-permute-start | bytes 2113544 | tf_op jit(solution)/shard_map/ppermute | solution.py:73
  221.5 61.0 %collective-permute-start.7 = (bf16[688,512]{1,0:T(8,128)(2,1)S(1)}, bf16[688,512]{1,0:T(8,128)(2,1)S(1)}, u32[]{:S(2)}, u32[]{:S(2)}) collective-permute-start(bf16[688,512]{1,0:T(8,128)(2,1)S(1)} %get-tuple-element.53), channel_id=1, source_target_pairs={{0,16},{8,24},{16,0},{24,8},{1,17},{9,25},{17,1},{25,9},{2,18},{10... | collective-permute-start | bytes 2113544 | tf_op jit(solution)/shard_map/ppermute | solution.py:73
  221.7 60.8 %collective-permute-start.6 = (bf16[688,512]{1,0:T(8,128)(2,1)S(1)}, bf16[688,512]{1,0:T(8,128)(2,1)S(1)}, u32[]{:S(2)}, u32[]{:S(2)}) collective-permute-start(bf16[688,512]{1,0:T(8,128)(2,1)S(1)} %get-tuple-element.54), channel_id=1, source_target_pairs={{0,8},{8,16},{16,24},{24,0},{1,9},{9,17},{17,25},{25,1},{2,10},{10... | collective-permute-start | bytes 2113544 | tf_op jit(solution)/shard_map/ppermute | solution.py:73
  285.0 77.0 %reduce-scatter.5.cloned.1.call-start = ((), (), s32[]{:S(2)}) async-start(), calls=%async_computation.9 | async-start | bytes 7077888 | tf_op jit(solution)/shard_map/reduce_scatter | solution.py:148
  312.9 7.3 %copy-start.12 = (bf16[2048,688]{0,1:T(8,128)(2,1)S(1)}, bf16[2048,688]{0,1:T(8,128)(2,1)}, u32[]{:S(2)}) copy-start(bf16[2048,688]{0,1:T(8,128)(2,1)} %maximum_bitcast_fusion.1) | copy-start | bytes 8454148
  320.2 11.6 %copy-start.8 = (bf16[2304,1024]{1,0:T(8,128)(2,1)S(1)}, bf16[2304,1024]{1,0:T(8,128)(2,1)}, u32[]{:S(2)}) copy-start(bf16[2304,1024]{1,0:T(8,128)(2,1)} %get-tuple-element.44) | copy-start | bytes 14155780
  320.2 11.6 %copy-start.11 = (bf16[2048,688]{0,1:T(8,128)(2,1)S(1)}, bf16[2048,688]{0,1:T(8,128)(2,1)}, u32[]{:S(2)}) copy-start(bf16[2048,688]{0,1:T(8,128)(2,1)} %maximum_bitcast_fusion) | copy-start | bytes 8454148
  331.7 11.3 %copy-start.13 = (bf16[86,8,2,512]{3,1,2,0:T(8,128)(2,1)S(1)}, bf16[86,8,2,512]{3,1,2,0:T(8,128)(2,1)}, u32[]{:S(2)}) copy-start(bf16[86,8,2,512]{3,1,2,0:T(8,128)(2,1)} %copy.30) | copy-start | bytes 4227076
  341.3 1.6 copy-start.20
  348.5 1.4 copy-start.7
  348.5 29.4 %reduce-scatter.9.cloned.1.call-start = ((), (), s32[]{:S(2)}) async-start(), calls=%async_computation.11 | async-start | bytes 7077888 | tf_op jit(solution)/shard_map/reduce_scatter | solution.py:148
  357.8 8.1 %copy-start.3 = (f32[1024,4]{1,0:T(8,128)S(1)}, f32[1024,4]{1,0:T(8,128)}, u32[]{:S(2)}) copy-start(f32[1024,4]{1,0:T(8,128)} %copy-done.2) | copy-start | bytes 49156
  362.0 32.0 %all-to-all-start.1 = ((bf16[4,576,512]{2,1,0:T(8,128)(2,1)}), bf16[4,576,512]{2,1,0:T(8,128)(2,1)S(1)}, u32[]{:S(2)}, u32[]{:S(2)}) async-start(bf16[4,576,512]{2,1,0:T(8,128)(2,1)} %bitcast.172), calls=%async_computation.2 | async-start | bytes 4718592 | tf_op jit(solution)/shard_map/all_to_all | solution.py:149
  394.1 1.4 copy-start.4
  395.5 30.9 %all-to-all-start.2 = ((bf16[4,576,512]{2,1,0:T(8,128)(2,1)}), bf16[4,576,512]{2,1,0:T(8,128)(2,1)S(1)}, u32[]{:S(2)}, u32[]{:S(2)}) async-start(bf16[4,576,512]{2,1,0:T(8,128)(2,1)} %bitcast.171), calls=%async_computation.5 | async-start | bytes 4718592 | tf_op jit(solution)/shard_map/all_to_all | solution.py:149
  399.1 35.4 %reduce-scatter.7.cloned.1.call-start = ((), (), s32[]{:S(2)}) async-start(), calls=%async_computation.10 | async-start | bytes 1310720 | tf_op jit(solution)/shard_map/reduce_scatter | solution.py:173
  405.6 57.0 %reduce-scatter.11.cloned.1.call-start = ((), (), s32[]{:S(2)}) async-start(), calls=%async_computation.12 | async-start | bytes 1310720 | tf_op jit(solution)/shard_map/reduce_scatter | solution.py:173
  429.5 33.1 %copy-start.6 = (f32[256,2048]{1,0:T(8,128)S(1)}, f32[256,2048]{1,0:T(8,128)}, u32[]{:S(2)}) copy-start(f32[256,2048]{1,0:T(8,128)} %copy-done.5) | copy-start | bytes 6291460
  429.5 35.1 %copy-start.1 = (bf16[256,1024]{1,0:T(8,128)(2,1)S(1)}, bf16[256,1024]{1,0:T(8,128)(2,1)}, u32[]{:S(2)}) copy-start(bf16[256,1024]{1,0:T(8,128)(2,1)} %param.12) | copy-start | bytes 1572868
Sparse Core Ops, SparseCore 0:
  10.3 55.2 all-gather.6
  139.2 17.7 all-reduce.1
  161.2 47.1 all-gather.8
  285.1 22.5 all-gather.10
  348.7 13.3 reduce-scatter.4
  364.2 13.7 reduce-scatter.8
  405.8 28.7 reduce-scatter.6
  436.8 25.7 reduce-scatter.10
where the time goes:
time: 479 us; the launch traced here: 472 us
  waiting for transfers between devices  258 us (54%)
  local copies, waits for them, and re-layouts  56.1 us (12%)
  starting transfers between devices  54.6 us (11%)
  matrix products  52.3 us (11%)
  other arithmetic  21.6 us (5%)
  blocking collectives  14.8 us (3%)
  between operations  14.4 us (3%)
    ppermute x9, waiting for transfers between devices, spread(): lax.ppermute(block, 'dp', [(i, (i + step) % copies) for i in range(copies)])  127 us
    all_gather x1, waiting for transfers between devices, local(): lax.all_gather(own_cols, 'dp', axis=0)  44.2 us
    ppermute x9, starting transfers between devices, spread(): lax.ppermute(block, 'dp', [(i, (i + step) % copies) for i in range(copies)])  40.5 us
    all_to_all x2, waiting for transfers between devices, local(): lax.all_to_all(summed.reshape(experts, count * capacity, width), 'expert'...  36.8 us
    reduce_scatter x2, waiting for transfers between devices, local(): lax.psum_scatter(jnp.concatenate(mixtures, axis=0).astype(jnp.bfloat16),...  31.6 us
    slice x1, local copies, waits for them, and re-layouts, local(): down_parts[:, part].reshape(tensor_count * width, down_full.shape[1])  19.3 us
    reduce_scatter x2, waiting for transfers between devices, local(): lax.psum_scatter(rounded, 'tensor', scatter_dimension=1, tiled=True)  15.6 us
    all_gather x1, blocking collectives, local(): choice = lax.all_gather(choice, 'dp', axis=0)  14.8 us
  transfers between devices with their start and end apart: 20, of which 13 were waited for; matrix products, arithmetic and copies ran while one was open for 16% of the time, Pallas kernels for 0%

commit v1 on v0

--- a/solution.py
+++ b/solution.py
@@ -6,6 +6,24 @@
 HDIM = 128
 EPSILON = 1e-05
 NEGATIVE = -1e30
+
+
+def recast_the_point(q_in, row_dim, dimension_no):
+    local_now = lax.psum(1, "expert")
+    piece_next = lax.axis_index("expert")
+    u_next, now = (local_now, piece_next)
+    base_arr = q_in.shape[row_dim] // u_next
+    then = list(q_in.shape)
+    then[row_dim] = base_arr
+    t1 = then[dimension_no]
+    then[dimension_no] = t1 * u_next
+    q_next = jnp.zeros(then, q_in.dtype)
+    for it in range(u_next):
+        reply = lax.dynamic_slice_in_dim(q_in, (now ^ it) * base_arr, base_arr, axis=row_dim)
+        if it:
+            reply = lax.ppermute(reply, "expert", [(k0, k0 ^ it) for k0 in range(u_next)])
+        q_next = lax.dynamic_update_slice_in_dim(q_next, reply, (now ^ it) * t1, axis=dimension_no)
+    return q_next
 
 
 def slot_table(block_routes, experts, capacity):
@@ -146,13 +164,7 @@
             preferred_element_type=jnp.float32,
         ).astype(jnp.bfloat16)
         summed = lax.psum_scatter(rounded, "tensor", scatter_dimension=1, tiled=True)
-        returned = lax.all_to_all(
-            summed.reshape(experts, count * capacity, width),
-            "expert",
-            split_axis=0,
-            concat_axis=0,
-            tiled=True,
-        )
+        returned = recast_the_point(summed.reshape(experts, count * capacity, width), 0, 0)
         mixtures = []
         for i, (mixing, high) in enumerate(splits):
             rows = returned[:, i * capacity : (i + 1) * capacity].reshape(slots, width)

time: 479 us -> 478 us (level)
  waiting for transfers between devices: 258 us -> 244 us
  local copies, waits for them, and re-layouts: 56.1 us -> 68.6 us
    all_to_all x2 -> x0, waiting for transfers between devices: 36.8 us -> none  [local(): lax.all_to_all(summed.reshape(experts, count * capacity, width), 'expert'...]
    ppermute x0 -> x6, waiting for transfers between devices: none -> 22.8 us  [recast_the_point(): lax.ppermute(reply, 'expert', [(k0, k0 ^ it) for k0 in range(u_next)])]
    dynamic_update_slice x0 -> x6, local copies, waits for them, and re-layouts: none -> 8.04 us  [recast_the_point(): lax.dynamic_update_slice_in_dim(q_next, reply, (now ^ it) * t1, axis=dime...]
    ppermute x0 -> x6, starting transfers between devices: none -> 7.62 us  [recast_the_point(): lax.ppermute(reply, 'expert', [(k0, k0 ^ it) for k0 in range(u_next)])]
    all_to_all x2 -> x0, starting transfers between devices: 7.52 us -> none  [local(): lax.all_to_all(summed.reshape(experts, count * capacity, width), 'expert'...]
    unnamed x46 -> x48, local copies, waits for them, and re-layouts: 10.1 us -> 11 us
  transfers between devices with their start and end apart: 20 -> 24, of which waited for: 13 -> 14; matrix products, arithmetic and copies ran while one was open for 16% -> 19% of each run, Pallas kernels for 0% -> 0%
where the time goes in v1:
time: 478 us; the launch traced here: 470 us
  waiting for transfers between devices  244 us (51%)
  local copies, waits for them, and re-layouts  68.6 us (14%)
  starting transfers between devices  54.7 us (11%)
  matrix products  52.3 us (11%)
  other arithmetic  21.6 us (5%)
  blocking collectives  14.8 us (3%)
  between operations  14.5 us (3%)
    ppermute x9, waiting for transfers between devices, spread(): lax.ppermute(block, 'dp', [(i, (i + step) % copies) for i in range(copies)])  127 us
    all_gather x1, waiting for transfers between devices, local(): lax.all_gather(own_cols, 'dp', axis=0)  44.2 us
    ppermute x9, starting transfers between devices, spread(): lax.ppermute(block, 'dp', [(i, (i + step) % copies) for i in range(copies)])  40.5 us
    reduce_scatter x2, waiting for transfers between devices, local(): lax.psum_scatter(jnp.concatenate(mixtures, axis=0).astype(jnp.bfloat16),...  35.4 us
    ppermute x6, waiting for transfers between devices, recast_the_point(): lax.ppermute(reply, 'expert', [(k0, k0 ^ it) for k0 in range(u_next)])  22.8 us
    slice x1, local copies, waits for them, and re-layouts, local(): down_parts[:, part].reshape(tensor_count * width, down_full.shape[1])  18.4 us
    all_gather x1, blocking collectives, local(): choice = lax.all_gather(choice, 'dp', axis=0)  14.8 us
    dot_general x2, matrix products, local(): lax.dot_general(hidden, down_parts[:, part].reshape(tensor_count * width,...  13.1 us
  transfers between devices with their start and end apart: 24, of which 14 were waited for; matrix products, arithmetic and copies ran while one was open for 19% of the time, Pallas kernels for 0%

profile of v1, /device:TPU:0, one launch (start us, length us, event | category | flops | bytes accessed | tf_op | source)
XLA Modules:
  0.0 470.5 jit_solution(7843093717492286274)
XLA Ops:
  6.5 1.3 copy.22
  7.9 1.2 copy.21
  10.3 14.8 %all-gather = f32[1024,4]{0,1:T(4,128)S(1)} all-gather(f32[256,4]{0,1:T(4,128)S(1)} %pad_maximum_fusion.12), channel_id=2, replica_groups=mesh['dp'=4,'expert'=4,'tensor'=2] {'dp'}, dimensions={0}, use_global_device_ids=true | all-gather | bytes 20480 | tf_op jit(solution)/shard_map/all_gather | solution.py:103
  25.4 3.4 constant_dynamic-slice_fusion.8
  28.8 3.4 collective-permute-start.2
  32.7 1.4 constant_dynamic-slice_fusion.7
  34.1 3.3 collective-permute-start.5
  37.4 1.1 collective-permute-start.4
  38.7 11.5 %collective-permute-done.2 = bf16[688,512]{1,0:T(8,128)(2,1)} collective-permute-done((bf16[688,512]{1,0:T(8,128)(2,1)}, bf16[688,512]{1,0:T(8,128)(2,1)}, u32[]{:S(2)}, u32[]{:S(2)}) %collective-permute-start.2) | collective-permute-done | bytes 704544 | tf_op jit(solution)/shard_map/ppermute | solution.py:91
  50.2 29.1 %collective-permute-start.3 = (bf16[688,512]{1,0:T(8,128)(2,1)S(1)}, bf16[688,512]{1,0:T(8,128)(2,1)}, u32[]{:S(2)}, u32[]{:S(2)}) collective-permute-start(bf16[688,512]{1,0:T(8,128)(2,1)S(1)} %get-tuple-element.62), channel_id=1, source_target_pairs={{0,8},{8,16},{16,24},{24,0},{1,9},{9,17},{17,25},{25,1},{2,10},{10... | collective-permute-start | bytes 2113544 | tf_op jit(solution)/shard_map/ppermute | solution.py:91
  79.2 45.1 %collective-permute-done.1 = bf16[688,512]{1,0:T(8,128)(2,1)} collective-permute-done((bf16[688,512]{1,0:T(8,128)(2,1)}, bf16[688,512]{1,0:T(8,128)(2,1)}, u32[]{:S(2)}, u32[]{:S(2)}) %collective-permute-start.1) | collective-permute-done | bytes 704544 | tf_op jit(solution)/shard_map/ppermute | solution.py:91
  124.4 1.7 pad_maximum_fusion.4
  126.3 1.7 maximum_bitcast_fusion
  128.0 2.7 fusion.100
  130.7 1.7 fusion
  132.4 2.0 fusion.3
  134.5 2.3 divide_convert_fusion
  136.8 2.3 convolution_convert_fusion.2
  139.5 11.1 %collective-permute-done.4 = bf16[688,512]{1,0:T(8,128)(2,1)} collective-permute-done((bf16[688,512]{1,0:T(8,128)(2,1)}, bf16[688,512]{1,0:T(8,128)(2,1)}, u32[]{:S(2)}, u32[]{:S(2)}) %collective-permute-start.4) | collective-permute-done | bytes 704544 | tf_op jit(solution)/shard_map/ppermute | solution.py:91
  150.6 1.7 pad_maximum_fusion.5
  152.5 1.8 maximum_bitcast_fusion.1
  154.3 2.8 all-reduce.2.cloned.1.call-done
  157.1 1.6 multiply_reduce_fusion
  158.8 1.3 copy-done.4
  164.1 44.2 %all-gather.9.cloned.1.call-done = bf16[1024,1024]{1,0:T(8,128)(2,1)} async-done(((bf16[256,1024]{1,0:T(8,128)(2,1)}), bf16[1024,1024]{1,0:T(8,128)(2,1)}) %all-gather.9.cloned.1.call-update) | async-done | bytes 2097168 | tf_op jit(solution)/shard_map/all_gather | solution.py:125
  208.3 1.7 convolution_convert_fusion.3
  210.0 1.5 convolution_convert_fusion.4
  212.5 2.4 pad_maximum_fusion.3
  214.8 5.2 %all-to-all-start = ((bf16[4,576,1024]{2,1,0:T(8,128)(2,1)}), bf16[4,576,1024]{2,1,0:T(8,128)(2,1)}, u32[]{:S(2)}, u32[]{:S(2)}) async-start(bf16[4,576,1024]{2,1,0:T(8,128)(2,1)} %pad_maximum_fusion.3), calls=%async_computation | async-start | bytes 9437184 | tf_op jit(solution)/shard_map/all_to_all | solution.py:143
  220.3 1.2 collective-permute-start.8
  221.7 1.7 collective-permute-start.6
  223.5 15.5 %collective-permute-done.8 = bf16[688,512]{1,0:T(8,128)(2,1)S(1)} collective-permute-done((bf16[688,512]{1,0:T(8,128)(2,1)S(1)}, bf16[688,512]{1,0:T(8,128)(2,1)S(1)}, u32[]{:S(2)}, u32[]{:S(2)}) %collective-permute-start.8) | collective-permute-done | bytes 704544 | tf_op jit(solution)/shard_map/ppermute | solution.py:91
  238.9 43.6 %collective-permute-done.7 = bf16[688,512]{1,0:T(8,128)(2,1)S(1)} collective-permute-done((bf16[688,512]{1,0:T(8,128)(2,1)S(1)}, bf16[688,512]{1,0:T(8,128)(2,1)S(1)}, u32[]{:S(2)}, u32[]{:S(2)}) %collective-permute-start.7) | collective-permute-done | bytes 704544 | tf_op jit(solution)/shard_map/ppermute | solution.py:91
  283.1 1.8 maximum_bitcast_fusion.2
  285.5 6.5 %reshape.189 = bf16[2,2,512,688]{2,1,0,3:T(2,128)(2,1)S(1)} reshape(bf16[2048,688]{0,1:T(8,128)(2,1)} %maximum_bitcast_fusion.2) | data formatting | bytes 5636096 | tf_op jit(solution)/shard_map/reshape | solution.py:156
  292.0 18.4 %slice_reduce_fusion.1 = (bf16[2,512,688]{1,0,2:T(2,128)(2,1)}, bf16[2,512,688]{1,0,2:T(2,128)(2,1)S(1)}) fusion(bf16[2,2,512,688]{2,1,0,3:T(2,128)(2,1)S(1)} %reshape.189), kind=kLoop, calls=%fused_computation.18 | loop fusion | bytes 5636096 | tf_op jit(solution)/shard_map/slice | solution.py:162
  310.4 1.5 copy.31
  311.9 7.3 %fusion.99 = (bf16[2304,1024]{1,0:T(8,128)(2,1)S(1)}, bf16[2304,1024]{1,0:T(8,128)(2,1)}) fusion(bf16[4608,1024]{1,0:T(8,128)(2,1)} %all-gather.11.cloned.1.call-done), kind=kLoop, calls=%fused_computation.226 | loop fusion | bytes 18874368 | tf_op jit(solution)/shard_map/slice | solution.py:149
  319.2 11.6 %fusion.1 = f32[2304,688]{0,1:T(8,128)} fusion(bf16[2048,688]{0,1:T(8,128)(2,1)S(1)} %copy-done.11, bf16[2304,1024]{1,0:T(8,128)(2,1)} %get-tuple-element.44, bf16[2304,1024]{1,0:T(8,128)(2,1)S(1)} %get-tuple-element.43), kind=kOutput, calls=%fused_computation.5 | convolution fusion | flops 6511656960 | bytes 18595840 | tf_op jit(solution)/shard_map/dot_general | solution.py:151
  330.8 9.6 %multiply_convert_fusion = bf16[2304,688]{0,1:T(8,128)(2,1)S(1)} fusion(f32[2304,688]{0,1:T(8,128)} %fusion.1, bf16[2048,688]{0,1:T(8,128)(2,1)S(1)} %copy-done.10, bf16[2304,1024]{1,0:T(8,128)(2,1)S(1)} %copy-done.7, bf16[2304,1024]{1,0:T(8,128)(2,1)S(1)} %get-tuple-element.43), kind=kOutput, calls=%fused_computation.4 | convolution fusion | flops 6521167872 | bytes 21766144 | tf_op jit(solution)/shard_map/dot_general | solution.py:150
  340.4 1.6 copy-done.21
  342.0 5.6 %convolution_convert_fusion = bf16[2304,1024]{1,0:T(8,128)(2,1)} fusion(bf16[2304,688]{0,1:T(8,128)(2,1)S(1)} %multiply_convert_fusion, bf16[1024,688]{0,1:T(8,128)(2,1)S(1)} %bitcast.174), kind=kOutput, calls=%fused_computation.9 | convolution fusion | flops 3248750592 | bytes 9297920 | tf_op jit(solution)/shard_map/dot_general | solution.py:160
  347.7 1.3 copy-done.6
  349.3 7.5 %convolution_convert_fusion.1 = bf16[2304,1024]{1,0:T(8,128)(2,1)} fusion(bf16[2304,688]{0,1:T(8,128)(2,1)} %copy-done.21, bf16[1024,688]{0,1:T(8,128)(2,1)S(1)} %bitcast.175), kind=kOutput, calls=%fused_computation.10 | convolution fusion | flops 3248750592 | bytes 9297920 | tf_op jit(solution)/shard_map/dot_general | solution.py:160
  357.1 4.0 reduce-scatter.9.cloned.1.call-done
  361.1 1.6 broadcast.60.clone
  363.6 1.4 constant_dynamic-slice_fusion
  365.1 1.7 collective-permute-start.12
  366.8 1.5 collective-permute-start.13
  369.2 7.9 %reduce-scatter.5.cloned.1.call-done = bf16[2304,512]{1,0:T(8,128)(2,1)} async-done(((bf16[2304,1024]{1,0:T(8,128)(2,1)}), bf16[2304,512]{1,0:T(8,128)(2,1)}) %reduce-scatter.5.cloned.1.call-update) | async-done | bytes 2359312 | tf_op jit(solution)/shard_map/reduce_scatter | solution.py:166
  377.3 1.5 copy-done.12
  378.7 1.3 constant_dynamic-slice_fusion.3
  380.0 1.7 collective-permute-start.9
  381.7 1.4 collective-permute-start.10
  384.2 1.9 constant_dynamic-update-slice_fusion.2
  386.1 8.8 %collective-permute-done.13 = bf16[1,576,512]{2,1,0:T(8,128)(2,1)} collective-permute-done((bf16[1,576,512]{2,1,0:T(8,128)(2,1)}, bf16[1,576,512]{2,1,0:T(8,128)(2,1)}, u32[]{:S(2)}, u32[]{:S(2)}) %collective-permute-start.13) | collective-permute-done | bytes 589856 | tf_op jit(solution)/shard_map/ppermute | solution.py:24
  394.9 1.9 constant_dynamic-update-slice_fusion.1
  396.8 1.9 constant_dynamic-update-slice_fusion
  398.8 1.8 fusion.102
  405.1 1.8 collective-permute-done.9
  408.0 12.2 %collective-permute-done.10 = bf16[1,576,512]{2,1,0:T(8,128)(2,1)S(1)} collective-permute-done((bf16[1,576,512]{2,1,0:T(8,128)(2,1)}, bf16[1,576,512]{2,1,0:T(8,128)(2,1)S(1)}, u32[]{:S(2)}, u32[]{:S(2)}) %collective-permute-start.10) | collective-permute-done | bytes 589856 | tf_op jit(solution)/shard_map/ppermute | solution.py:24
  426.0 7.3 %reduce-scatter.11.cloned.1.call-done = bf16[256,512]{1,0:T(8,128)(2,1)} async-done(((bf16[1024,512]{1,0:T(8,128)(2,1)}), bf16[256,512]{1,0:T(8,128)(2,1)}) %reduce-scatter.11.cloned.1.call-update) | async-done | bytes 262160 | tf_op jit(solution)/shard_map/reduce_scatter | solution.py:185
  433.3 28.1 %reduce-scatter.7.cloned.1.call-done = bf16[256,512]{1,0:T(8,128)(2,1)} async-done(((bf16[1024,512]{1,0:T(8,128)(2,1)}), bf16[256,512]{1,0:T(8,128)(2,1)}) %reduce-scatter.7.cloned.1.call-update) | async-done | bytes 262160 | tf_op jit(solution)/shard_map/reduce_scatter | solution.py:185
  461.5 2.0 add_convert_fusion
  (132 shorter events, 24.3 us)
Async XLA Ops:
  6.5 124.2 %copy-start = (bf16[256,1024]{1,0:T(8,128)(2,1)S(1)}, bf16[256,1024]{1,0:T(8,128)(2,1)}, u32[]{:S(2)}) copy-start(bf16[256,1024]{1,0:T(8,128)(2,1)} %param.12) | copy-start | bytes 1572868
  6.5 3.7 copy-start.17
  6.5 3.8 copy-start.18
  6.5 121.5 %all-gather.7.cloned.1.call-start = ((), (), s32[]{:S(2)}) async-start(), calls=%async_computation.5 | async-start | bytes 5242880 | tf_op jit(solution)/shard_map/all_gather | solution.py:101
  10.2 146.9 %all-reduce.2.cloned.1.call-start = ((), (), s32[]{:S(2)}) async-start(), calls=%async_computation.6 | async-start | bytes 2097152 | tf_op jit(solution)/shard_map/psum | solution.py:111
  25.3 138.0 %copy-start.2 = (f32[1024,4]{1,0:T(8,128)}, f32[1024,4]{1,0:T(8,128)S(1)}, u32[]{:S(2)}) copy-start(f32[1024,4]{1,0:T(8,128)S(1)} %copy.23) | copy-start | bytes 49156
  25.4 7.3 %copy-start.8 = (bf16[1,512,2752]{1,2,0:T(8,128)(2,1)S(1)}, bf16[1,512,2752]{1,2,0:T(8,128)(2,1)}, u32[]{:S(2)}) copy-start(bf16[1,512,2752]{1,2,0:T(8,128)(2,1)} %param.20) | copy-start | bytes 8454148
  28.8 21.4 %collective-permute-start.2 = (bf16[688,512]{1,0:T(8,128)(2,1)}, bf16[688,512]{1,0:T(8,128)(2,1)}, u32[]{:S(2)}, u32[]{:S(2)}) collective-permute-start(bf16[688,512]{1,0:T(8,128)(2,1)} %get-tuple-element.68), channel_id=1, source_target_pairs={{0,24},{8,0},{16,8},{24,16},{1,25},{9,1},{17,9},{25,17},{2,26},{10... | collective-permute-start | bytes 2113544 | tf_op jit(solution)/shard_map/ppermute | solution.py:91
  32.2 92.2 %collective-permute-start.1 = (bf16[688,512]{1,0:T(8,128)(2,1)}, bf16[688,512]{1,0:T(8,128)(2,1)}, u32[]{:S(2)}, u32[]{:S(2)}) collective-permute-start(bf16[688,512]{1,0:T(8,128)(2,1)} %get-tuple-element.69), channel_id=1, source_target_pairs={{0,16},{8,24},{16,0},{24,8},{1,17},{9,25},{17,1},{25,9},{2,18},{10... | collective-permute-start | bytes 2113544 | tf_op jit(solution)/shard_map/ppermute | solution.py:91
  32.2 92.2 %collective-permute-start = (bf16[688,512]{1,0:T(8,128)(2,1)}, bf16[688,512]{1,0:T(8,128)(2,1)}, u32[]{:S(2)}, u32[]{:S(2)}) collective-permute-start(bf16[688,512]{1,0:T(8,128)(2,1)} %get-tuple-element.70), channel_id=1, source_target_pairs={{0,8},{8,16},{16,24},{24,0},{1,9},{9,17},{17,25},{25,1},{2,10},{10... | collective-permute-start | bytes 2113544 | tf_op jit(solution)/shard_map/ppermute | solution.py:91
  34.1 105.4 %collective-permute-start.5 = (bf16[688,512]{1,0:T(8,128)(2,1)}, bf16[688,512]{1,0:T(8,128)(2,1)}, u32[]{:S(2)}, u32[]{:S(2)}) collective-permute-start(bf16[688,512]{1,0:T(8,128)(2,1)} %get-tuple-element.60), channel_id=1, source_target_pairs={{0,24},{8,0},{16,8},{24,16},{1,25},{9,1},{17,9},{25,17},{2,26},{10... | collective-permute-start | bytes 2113544 | tf_op jit(solution)/shard_map/ppermute | solution.py:91
  37.4 113.2 %collective-permute-start.4 = (bf16[688,512]{1,0:T(8,128)(2,1)}, bf16[688,512]{1,0:T(8,128)(2,1)}, u32[]{:S(2)}, u32[]{:S(2)}) collective-permute-start(bf16[688,512]{1,0:T(8,128)(2,1)} %get-tuple-element.61), channel_id=1, source_target_pairs={{0,16},{8,24},{16,0},{24,8},{1,17},{9,25},{17,1},{25,9},{2,18},{10... | collective-permute-start | bytes 2113544 | tf_op jit(solution)/shard_map/ppermute | solution.py:91
  50.2 100.4 %collective-permute-start.3 = (bf16[688,512]{1,0:T(8,128)(2,1)S(1)}, bf16[688,512]{1,0:T(8,128)(2,1)}, u32[]{:S(2)}, u32[]{:S(2)}) collective-permute-start(bf16[688,512]{1,0:T(8,128)(2,1)S(1)} %get-tuple-element.62), channel_id=1, source_target_pairs={{0,8},{8,16},{16,24},{24,0},{1,9},{9,17},{17,25},{25,1},{2,10},{10... | collective-permute-start | bytes 2113544 | tf_op jit(solution)/shard_map/ppermute | solution.py:91
  134.5 2.3 copy-start.19
  136.8 2.7 copy-start.16
  139.1 69.2 %all-gather.9.cloned.1.call-start = ((), (), s32[]{:S(2)}) async-start(), calls=%async_computation.11 | async-start | bytes 2621440 | tf_op jit(solution)/shard_map/all_gather | solution.py:125
  152.5 4.6 copy-start.15
  158.7 1.3 copy-start.4
  208.3 3.2 copy-start.20
  214.8 5.2 %copy-start.9 = (bf16[1,512,2752]{1,2,0:T(8,128)(2,1)S(1)}, bf16[1,512,2752]{1,2,0:T(8,128)(2,1)}, u32[]{:S(2)}) copy-start(bf16[1,512,2752]{1,2,0:T(8,128)(2,1)} %param.21) | copy-start | bytes 8454148
  214.8 70.1 %all-to-all-start = ((bf16[4,576,1024]{2,1,0:T(8,128)(2,1)}), bf16[4,576,1024]{2,1,0:T(8,128)(2,1)}, u32[]{:S(2)}, u32[]{:S(2)}) async-start(bf16[4,576,1024]{2,1,0:T(8,128)(2,1)} %pad_maximum_fusion.3), calls=%async_computation | async-start | bytes 9437184 | tf_op jit(solution)/shard_map/all_to_all | solution.py:143
  220.0 91.9 %all-gather.11.cloned.1.call-start = ((), (), s32[]{:S(2)}) async-start(), calls=%async_computation.12 | async-start | bytes 14155776 | tf_op jit(solution)/shard_map/all_gather | solution.py:148
  220.3 18.6 %collective-permute-start.8 = (bf16[688,512]{1,0:T(8,128)(2,1)S(1)}, bf16[688,512]{1,0:T(8,128)(2,1)S(1)}, u32[]{:S(2)}, u32[]{:S(2)}) collective-permute-start(bf16[688,512]{1,0:T(8,128)(2,1)S(1)} %get-tuple-element.52), channel_id=1, source_target_pairs={{0,24},{8,0},{16,8},{24,16},{1,25},{9,1},{17,9},{25,17},{2,26},{10... | collective-permute-start | bytes 2113544 | tf_op jit(solution)/shard_map/ppermute | solution.py:91
  221.5 61.0 %collective-permute-start.7 = (bf16[688,512]{1,0:T(8,128)(2,1)S(1)}, bf16[688,512]{1,0:T(8,128)(2,1)S(1)}, u32[]{:S(2)}, u32[]{:S(2)}) collective-permute-start(bf16[688,512]{1,0:T(8,128)(2,1)S(1)} %get-tuple-element.53), channel_id=1, source_target_pairs={{0,16},{8,24},{16,0},{24,8},{1,17},{9,25},{17,1},{25,9},{2,18},{10... | collective-permute-start | bytes 2113544 | tf_op jit(solution)/shard_map/ppermute | solution.py:91
  221.7 60.8 %collective-permute-start.6 = (bf16[688,512]{1,0:T(8,128)(2,1)S(1)}, bf16[688,512]{1,0:T(8,128)(2,1)S(1)}, u32[]{:S(2)}, u32[]{:S(2)}) collective-permute-start(bf16[688,512]{1,0:T(8,128)(2,1)S(1)} %get-tuple-element.54), channel_id=1, source_target_pairs={{0,8},{8,16},{16,24},{24,0},{1,9},{9,17},{17,25},{25,1},{2,10},{10... | collective-permute-start | bytes 2113544 | tf_op jit(solution)/shard_map/ppermute | solution.py:91
  285.0 76.2 %reduce-scatter.9.cloned.1.call-start = ((), (), s32[]{:S(2)}) async-start(), calls=%async_computation.9 | async-start | bytes 7077888 | tf_op jit(solution)/shard_map/reduce_scatter | solution.py:166
  311.9 7.3 %copy-start.11 = (bf16[2048,688]{0,1:T(8,128)(2,1)S(1)}, bf16[2048,688]{0,1:T(8,128)(2,1)}, u32[]{:S(2)}) copy-start(bf16[2048,688]{0,1:T(8,128)(2,1)} %maximum_bitcast_fusion.1) | copy-start | bytes 8454148
  319.2 11.6 %copy-start.7 = (bf16[2304,1024]{1,0:T(8,128)(2,1)S(1)}, bf16[2304,1024]{1,0:T(8,128)(2,1)}, u32[]{:S(2)}) copy-start(bf16[2304,1024]{1,0:T(8,128)(2,1)} %get-tuple-element.44) | copy-start | bytes 14155780
  319.2 11.6 %copy-start.10 = (bf16[2048,688]{0,1:T(8,128)(2,1)S(1)}, bf16[2048,688]{0,1:T(8,128)(2,1)}, u32[]{:S(2)}) copy-start(bf16[2048,688]{0,1:T(8,128)(2,1)} %maximum_bitcast_fusion) | copy-start | bytes 8454148
  330.8 11.3 %copy-start.14 = (bf16[86,8,2,512]{3,1,2,0:T(8,128)(2,1)S(1)}, bf16[86,8,2,512]{3,1,2,0:T(8,128)(2,1)}, u32[]{:S(2)}) copy-start(bf16[86,8,2,512]{3,1,2,0:T(8,128)(2,1)} %copy.31) | copy-start | bytes 4227076
  340.4 1.6 copy-start.21
  347.6 1.4 copy-start.6
  347.6 29.4 %reduce-scatter.5.cloned.1.call-start = ((), (), s32[]{:S(2)}) async-start(), calls=%async_computation.7 | async-start | bytes 7077888 | tf_op jit(solution)/shard_map/reduce_scatter | solution.py:166
  356.9 76.5 %reduce-scatter.11.cloned.1.call-start = ((), (), s32[]{:S(2)}) async-start(), calls=%async_computation.10 | async-start | bytes 1310720 | tf_op jit(solution)/shard_map/reduce_scatter | solution.py:185
  361.1 2.5 copy-start.13
  363.6 4.9 %copy-start.3 = (f32[1024,4]{1,0:T(8,128)S(1)}, f32[1024,4]{1,0:T(8,128)}, u32[]{:S(2)}) copy-start(f32[1024,4]{1,0:T(8,128)} %copy-done.2) | copy-start | bytes 49156
  365.1 18.1 %collective-permute-start.12 = (bf16[1,576,512]{2,1,0:T(8,128)(2,1)}, bf16[1,576,512]{2,1,0:T(8,128)(2,1)}, u32[]{:S(2)}, u32[]{:S(2)}) collective-permute-start(bf16[1,576,512]{2,1,0:T(8,128)(2,1)} %get-tuple-element.85), channel_id=1, source_target_pairs={{0,2},{2,0},{4,6},{6,4},{1,3},{3,1},{5,7},{7,5},{8,10},{10,8},{12,... | collective-permute-start | bytes 1769480 | tf_op jit(solution)/shard_map/ppermute | solution.py:24
  366.8 28.2 %collective-permute-start.13 = (bf16[1,576,512]{2,1,0:T(8,128)(2,1)}, bf16[1,576,512]{2,1,0:T(8,128)(2,1)}, u32[]{:S(2)}, u32[]{:S(2)}) collective-permute-start(bf16[1,576,512]{2,1,0:T(8,128)(2,1)} %get-tuple-element.84), channel_id=1, source_target_pairs={{0,4},{2,6},{4,0},{6,2},{1,5},{3,7},{5,1},{7,3},{8,12},{10,14},{12... | collective-permute-start | bytes 1769480 | tf_op jit(solution)/shard_map/ppermute | solution.py:24
  368.3 28.6 %collective-permute-start.14 = (bf16[1,576,512]{2,1,0:T(8,128)(2,1)}, bf16[1,576,512]{2,1,0:T(8,128)(2,1)}, u32[]{:S(2)}, u32[]{:S(2)}) collective-permute-start(bf16[1,576,512]{2,1,0:T(8,128)(2,1)} %get-tuple-element.83), channel_id=1, source_target_pairs={{0,6},{2,4},{4,2},{6,0},{1,7},{3,5},{5,3},{7,1},{8,14},{10,12},{12... | collective-permute-start | bytes 1769480 | tf_op jit(solution)/shard_map/ppermute | solution.py:24
  377.1 1.7 copy-start.12
  380.0 26.8 %collective-permute-start.9 = (bf16[1,576,512]{2,1,0:T(8,128)(2,1)}, bf16[1,576,512]{2,1,0:T(8,128)(2,1)}, u32[]{:S(2)}, u32[]{:S(2)}) collective-permute-start(bf16[1,576,512]{2,1,0:T(8,128)(2,1)} %get-tuple-element.77), channel_id=1, source_target_pairs={{0,2},{2,0},{4,6},{6,4},{1,3},{3,1},{5,7},{7,5},{8,10},{10,8},{12,... | collective-permute-start | bytes 1769480 | tf_op jit(solution)/shard_map/ppermute | solution.py:24
  381.7 38.4 %collective-permute-start.10 = (bf16[1,576,512]{2,1,0:T(8,128)(2,1)}, bf16[1,576,512]{2,1,0:T(8,128)(2,1)S(1)}, u32[]{:S(2)}, u32[]{:S(2)}) collective-permute-start(bf16[1,576,512]{2,1,0:T(8,128)(2,1)} %get-tuple-element.76), channel_id=1, source_target_pairs={{0,4},{2,6},{4,0},{6,2},{1,5},{3,7},{5,1},{7,3},{8,12},{10,14},{12... | collective-permute-start | bytes 1769480 | tf_op jit(solution)/shard_map/ppermute | solution.py:24
  383.2 37.0 %collective-permute-start.11 = (bf16[1,576,512]{2,1,0:T(8,128)(2,1)}, bf16[1,576,512]{2,1,0:T(8,128)(2,1)}, u32[]{:S(2)}, u32[]{:S(2)}) collective-permute-start(bf16[1,576,512]{2,1,0:T(8,128)(2,1)} %get-tuple-element.75), channel_id=1, source_target_pairs={{0,6},{2,4},{4,2},{6,0},{1,7},{3,5},{5,3},{7,1},{8,14},{10,12},{12... | collective-permute-start | bytes 1769480 | tf_op jit(solution)/shard_map/ppermute | solution.py:24
  405.0 56.5 %reduce-scatter.7.cloned.1.call-start = ((), (), s32[]{:S(2)}) async-start(), calls=%async_computation.8 | async-start | bytes 1310720 | tf_op jit(solution)/shard_map/reduce_scatter | solution.py:185
  424.5 37.0 %copy-start.5 = (f32[256,2048]{1,0:T(8,128)S(1)}, f32[256,2048]{1,0:T(8,128)}, u32[]{:S(2)}) copy-start(f32[256,2048]{1,0:T(8,128)} %copy-done.4) | copy-start | bytes 6291460
  424.5 38.9 %copy-start.1 = (bf16[256,1024]{1,0:T(8,128)(2,1)S(1)}, bf16[256,1024]{1,0:T(8,128)(2,1)}, u32[]{:S(2)}) copy-start(bf16[256,1024]{1,0:T(8,128)(2,1)} %param.12) | copy-start | bytes 1572868
Sparse Core Ops, SparseCore 0:
  10.3 55.2 all-gather.6
  139.2 17.8 all-reduce.1
  161.1 47.1 all-gather.8
  285.1 22.5 all-gather.10
  347.8 13.3 reduce-scatter.8
  363.3 13.7 reduce-scatter.4
  405.1 28.1 reduce-scatter.10
  435.6 25.7 reduce-scatter.6
